TPU v7x, 512 devices: a whole 4x8x8 slice. The times are simulated.
512 devices in a mesh: dp: 32 (over x, z), mp: 16 (over y, core).
Axes of the slice: x: 4, y: 8, z: 8, core: 2. Of those that a mesh axis runs over, the one named last changes fastest.
Arguments:
- inputs: bfloat16 [32, 1024, 2560], P('dp', 'mp'), may hold values from -6 to 6
- out_grads: bfloat16 [32, 1024, 5120], P('dp', None, 'mp'), may hold values from -6 to 6
- counts: int32 [32, 1024], P('dp'), may hold values from 1 to 16
- residual: bfloat16 [32, 2560, 5120], P('dp', None, 'mp'), may hold values from -3 to 3
- q_start: float32 [5120, 32], P('mp'), may hold values from -6 to 6
Outputs:
- update: bfloat16 [2560, 5120], P('dp', 'mp')
- residual_next: bfloat16 [32, 2560, 5120], P('dp', None, 'mp')
- q_next: float32 [5120, 32], P('mp')
All inputs are finite; a program needn't handle non-finite values.
Results may differ from a plain program's by a relative error of at most 0.0055.
Values may be sent and summed in bfloat16 or wider, within the bound.
A program may use at most 64 MiB of HBM per device.

v0:
```python
import math

import jax
import jax.numpy as jnp
from jax import lax
from jax.sharding import PartitionSpec as P

DIVISOR = 8


def reduce_factor(p_partial):
    p_sum = lax.psum(p_partial, ("dp", "mp"))
    gram_matrix = jnp.dot(p_sum.T, p_sum, precision=lax.Precision.HIGHEST)
    factor = jnp.linalg.cholesky(gram_matrix)
    p_hat = lax.linalg.triangular_solve(
        factor, p_sum, left_side=False, lower=True, transpose_a=True
    )
    return p_hat


def local(inputs, out_grads, counts, residual, q_start):
    token_count = out_grads.shape[1]
    feature_rows = inputs.shape[2]
    scaling = 1.0 / math.sqrt(token_count)
    weighted = (
        out_grads[0].astype(jnp.float32) * (counts[0].astype(jnp.float32) / DIVISOR)[:, None]
    ).astype(jnp.bfloat16)
    residual_local = residual[0].astype(jnp.float32)
    gradient = lax.dot_general(
        lax.all_gather(inputs, "mp", axis=1, tiled=True)[0],
        weighted,
        (((0,), (0,)), ((), ())),
        preferred_element_type=jnp.float32,
    )
    merged = gradient * scaling + residual_local
    p_partial = jnp.dot(merged, q_start, precision=lax.Precision.HIGHEST)
    p_hat = reduce_factor(p_partial)
    q_partial = jnp.dot(merged.T, p_hat, precision=lax.Precision.HIGHEST)
    q_next = lax.psum(q_partial, "dp")
    approx = jnp.dot(p_hat, q_next.T, precision=lax.Precision.HIGHEST)
    replicas = lax.axis_size("dp")
    row_count = feature_rows // replicas
    update = lax.dynamic_slice_in_dim(
        approx, lax.axis_index("dp") * row_count, row_count, 0
    ).astype(jnp.bfloat16)
    residual_next = (merged - approx / replicas).astype(jnp.bfloat16)[None]
    return (update, residual_next, q_next)


def solution(mesh):
    return jax.shard_map(
        local,
        mesh=mesh,
        in_specs=(
            P("dp", "mp", None),
            P("dp", None, "mp"),
            P("dp", None),
            P("dp", None, "mp"),
            P("mp", None),
        ),
        out_specs=(P("dp", "mp"), P("dp", None, "mp"), P("mp", None)),
        check_vma=False,
    )
```

profile of v0, /device:TPU:32, one launch (start us, length us, event | category | flops | bytes accessed | tf_op | source)
XLA Modules:
  0.0 503.4 jit_solution(3454755927091546072)
XLA Ops:
  7.2 0.0 copy-start
  7.2 0.0 all-gather.2.cloned.1.call-start
  7.2 0.7 all-gather.2.cloned.1.call-update
  7.9 0.0 all-reduce.2.cloned.1.call-start
  8.0 0.7 convert_multiply_fusion
  8.7 49.3 %all-gather.2.cloned.1.call-done = bf16[1,1024,2560]{2,1,0:T(8,128)(2,1)} async-done(((bf16[1,64,2560]{2,1,0:T(8,128)(2,1)}), bf16[1,1024,2560]{2,1,0:T(8,128)(2,1)}) %all-gather.2.cloned.1.call-update) | async-done | bytes 5242896 | tf_op jit(solution)/shard_map/all_gather | solution.py:30
  57.9 5.0 %fusion.8 = f32[2560,320]{0,1:T(8,128)S(1)} fusion(bf16[1,1024,2560]{2,1,0:T(8,128)(2,1)} %all-gather.2.cloned.1.call-done, bf16[1,2560,320]{1,2,0:T(8,128)(2,1)} %param.8, bf16[1,1024,320]{1,2,0:T(8,128)(2,1)} %param.6, f32[1024]{0:T(1024)S(1)} %bitcast.40), kind=kOutput, calls=%fused_computation.4 | convolution fusion | flops 1681162240 | bytes 10817536 | tf_op jit(solution)/shard_map/dot_general | solution.py:29
  63.0 0.0 copy-done
  63.0 2.9 fusion.19
  65.9 0.0 all-reduce.2.cloned.1.call-update
  65.9 269.5 %all-reduce.2.cloned.1.call-done = f32[2560,32]{0,1:T(8,128)} async-done(((f32[2560,32]{0,1:T(8,128)}), f32[2560,32]{0,1:T(8,128)}) %all-reduce.2.cloned.1.call-update) | async-done | bytes 327696 | tf_op jit(solution)/shard_map/psum | solution.py:12
  335.4 1.5 fusion.20
  336.9 0.1 copy.8
  337.0 2.9 cholesky.16
  339.9 0.6 compare_reduce_fusion
  340.6 0.7 fusion.15
  341.2 2.4 custom-call.6
  343.7 1.5 fusion.16
  345.1 0.0 copy-start.1
  345.1 0.7 copy-done.1
  345.9 2.8 fusion.21
  348.6 141.5 %psum.15 = f32[320,32]{0,1:T(8,128)S(1)} all-reduce(f32[320,32]{0,1:T(8,128)S(1)} %fusion.21), channel_id=1, replica_groups=mesh['dp'=32,'mp'=16] {'dp'}, use_global_device_ids=true, to_apply=%region_3.4 | all-reduce | flops 10240 | bytes 81920 | tf_op jit(solution)/shard_map/psum | solution.py:39
  490.1 0.0 copy-start.2
  490.1 3.7 fusion.22
  493.8 1.9 fusion.11
  495.7 0.0 copy-done.2
  495.7 0.1 dynamic-slice_convert_fusion
  495.8 0.7 copy.9
  (2 shorter events, 0.0 us)
Async XLA Ops:
  7.2 55.8 %copy-start = (f32[320,32]{0,1:T(8,128)S(1)}, f32[320,32]{0,1:T(8,128)}, u32[]{:S(2)}) copy-start(f32[320,32]{0,1:T(8,128)} %param.9) | copy-start | bytes 122884
  7.2 50.7 %all-gather.2.cloned.1.call-start = ((), (), s32[]{:S(2)}) async-start(), calls=%async_computation | async-start | bytes 5570560 | tf_op jit(solution)/shard_map/all_gather | solution.py:30
  7.9 327.5 %all-reduce.2.cloned.1.call-start = ((), (), s32[]{:S(2)}) async-start(), calls=%async_computation.1 | async-start | bytes 655360 | tf_op jit(solution)/shard_map/psum | solution.py:12
  345.1 0.7 copy-start.1
  490.1 5.6 %copy-start.2 = (f32[320,32]{0,1:T(8,128)}, f32[320,32]{0,1:T(8,128)S(1)}, u32[]{:S(2)}) copy-start(f32[320,32]{0,1:T(8,128)S(1)} %psum.15) | copy-start | bytes 122884
Sparse Core Ops, SparseCore 0:
  10.1 47.7 all-gather.1
  66.0 269.3 all-reduce.1
where the time goes:
time: 504 us; the launch traced here: 503 us
  waiting for transfers between devices  320 us (63%)
  blocking collectives  141 us (28%)
  matrix products  17.3 us (3%)
  between operations  14.1 us (3%)
  other arithmetic  9.25 us (2%)
    psum x1, waiting for transfers between devices, reduce_factor(): p_sum = lax.psum(p_partial, ('dp', 'mp'))  270 us
    psum x1, blocking collectives, local(): q_next = lax.psum(q_partial, 'dp')  141 us
    all_gather x1, waiting for transfers between devices, local(): lax.all_gather(inputs, 'mp', axis=1, tiled=True)[0]  49.3 us
  transfers between devices with their start and end apart: 2, of which 2 were waited for; matrix products, arithmetic and copies ran while one was open for 0% of the time, Pallas kernels for 0%

commit v1 on v0

v1 whole, which is shorter than its diff:
```python
import functools

import jax
import jax.numpy as jnp
from jax import lax
from jax.experimental import pallas as pl
from jax.experimental.pallas import tpu as pltpu
from jax.sharding import PartitionSpec as P

MESH = pl.DeviceIdType.MESH
F32, BF16 = jnp.float32, jnp.bfloat16
NX, NY, NZ, NC = 4, 8, 8, 2
ROWS, COLS, RANK, TOK = 2560, 320, 32, 1024
HALF = RANK // NC
BLOCK = TOK // (NY * NC)
PAIR = BLOCK * NC
XL = ROWS // NX
ZR = HALF // NZ
QR = RANK // NX
QL = 384
SUB = BLOCK // 2
SCALE = 1.0 / 32.0
DIVISOR = 8.0
NT = (((1,), (1,)), ((), ()))
NN = (((1,), (0,)), ((), ()))
TN = (((0,), (0,)), ((), ()))


def dot(a, b, dims):
    return lax.dot_general(a, b, dims, preferred_element_type=F32)


def dot_exact(a, b, dims):
    return lax.dot_general(a, b, dims, precision=lax.Precision.HIGHEST, preferred_element_type=F32)


def split3(v):
    high = v.astype(BF16)
    rest = v - high.astype(F32)
    mid = rest.astype(BF16)
    low = (rest - mid.astype(F32)).astype(BF16)
    return jnp.concatenate([high, mid, low], axis=0)


def sum3(v):
    n = v.shape[0] // 3
    return v[:n] + (v[n : 2 * n] + v[2 * n :])


def inverse_factor(gram):
    rows = lax.broadcasted_iota(jnp.int32, (RANK, 128), 0)
    lanes = lax.broadcasted_iota(jnp.int32, (RANK, 128), 1)
    eye = jnp.where(lanes == rows + RANK, 1.0, 0.0)
    work = jnp.concatenate([gram, jnp.zeros((RANK, 128 - RANK), F32)], axis=1) + eye

    def step(j, m):
        row = jnp.sum(jnp.where(rows == j, m, 0.0), axis=0, keepdims=True)
        col = jnp.sum(jnp.where(lanes == j, m, 0.0), axis=1, keepdims=True)
        pivot = jnp.sum(jnp.where(lanes[:1] == j, row, 0.0), axis=1, keepdims=True)
        inv = 1.0 / jnp.sqrt(pivot)
        row = row * inv
        return jnp.where(rows > j, m - (col * inv) * row, jnp.where(rows == j, row, m))

    return lax.fori_loop(0, RANK, step, work)[:, RANK : 2 * RANK]


def chain_kernel(
    inp_hbm, og_hbm, cnt_hbm, res_hbm, q_hbm,
    merged_hbm, phat_ref, qnext_ref,
    gbuf, og, cnt, res, q, wbuf, merged,
    wq, wqin, wqh, wqr, rq, rqin, ph, xr, p1, zs, zr, yr, zg, pa, pt,
    qb, qxr, qzr, qt,
    lsem, gsend, grecv, csend, crecv, cown, esend, erecv,
    wsend, wrecv, xsend, xrecv, zsend, zrecv, ysend, yrecv,
    zgsend, zgrecv, xgsend, xgrecv, qxsend, qxrecv, qzsend, qzrecv, qgsend, qgrecv,
):
    dp, mp = lax.axis_index("dp"), lax.axis_index("mp")
    x, z = dp // NZ, lax.rem(dp, NZ)
    y, c = mp // NC, lax.rem(mp, NC)

    def at_x(i):
        return (i * NZ + z, mp)

    def at_z(i):
        return (x * NZ + i, mp)

    def at_y(i):
        return (dp, i * NC + c)

    sibling = (dp, y * NC + (1 - c))

    def other(i, d, n):
        return lax.rem(i + d, n)

    def copy(src, dst, s, r, to):
        return pltpu.make_async_remote_copy(src, dst, s, r, device_id=to, device_id_type=MESH)

    loads = [
        pltpu.make_async_copy(og_hbm, og, lsem.at[0]),
        pltpu.make_async_copy(cnt_hbm, cnt, lsem.at[1]),
        pltpu.make_async_copy(q_hbm, q, lsem.at[2]),
        pltpu.make_async_copy(inp_hbm, gbuf.at[mp], lsem.at[3]),
        pltpu.make_async_copy(res_hbm, res, lsem.at[4]),
    ]
    for load in loads:
        load.start()

    barrier = pltpu.get_barrier_semaphore()
    peers = [sibling]
    peers += [at_x(other(x, d, NX)) for d in range(1, NX)]
    peers += [at_z(other(z, d, NZ)) for d in range(1, NZ)]
    peers += [at_y(other(y, d, NY)) for d in range(1, NY)]
    for peer in peers:
        pl.semaphore_signal(barrier, inc=1, device_id=peer, device_id_type=MESH)

    loads[0].wait()
    loads[1].wait()
    loads[2].wait()
    weight = jnp.broadcast_to(cnt[...].astype(F32) / DIVISOR, (8, TOK)).T[:, 0:1]
    wbuf[...] = (og[...].astype(F32) * weight).astype(BF16)
    q3 = split3(q[...].T)
    wq[...] = sum3(dot(q3, wbuf[...], NT)).reshape(NC, HALF, TOK)
    pl.semaphore_wait(barrier, len(peers))

    pending = []

    def go(cp):
        cp.start()
        pending.append(cp)
        return cp

    w_ex = go(copy(wq.at[1 - c], wqin, esend.at[0], erecv.at[0], sibling))
    loads[3].wait()
    own_ex = go(copy(gbuf.at[mp], gbuf.at[mp], esend.at[1], cown, sibling))
    w_ex.wait_recv()
    wqh[...] = wq[c] + wqin[...]
    for d in range(1, NY):
        i = other(y, d, NY)
        go(copy(wqh.at[:, pl.ds(pl.multiple_of(i * PAIR, PAIR), PAIR)], wqr.at[y], wsend.at[d], wrecv.at[y], at_y(i)))

    def ring_block(up, h):
        return lax.rem(y + (NY - h if up else h), NY) * NC + c

    def ring_send(up, h, s):
        part = gbuf.at[ring_block(up, h), pl.ds(s * SUB, SUB)]
        to = at_y(other(y, 1 if up else NY - 1, NY))
        u = 0 if up else 1
        go(copy(part, part, gsend.at[u, h, s], grecv.at[u, h, s], to))

    def ring_recv(up, h, s):
        part = gbuf.at[ring_block(up, h), pl.ds(s * SUB, SUB)]
        u = 0 if up else 1
        copy(part, part, gsend.at[u, h - 1, s], grecv.at[u, h - 1, s], sibling).wait_recv()
        go(copy(part, part, csend.at[u, h - 1, s], crecv.at[u, h - 1, s], sibling))

    def ring_step(h, s):
        for up in (True, False):
            if h == NY // 2 and (s == 0) != up:
                continue
            ring_recv(up, h, s)
            if h < NY // 2 - 1 or (h == NY // 2 - 1 and (s == 0) == up):
                ring_send(up, h, s)

    for s in range(2):
        ring_send(True, 0, s)
        ring_send(False, 0, s)

    loads[4].wait()
    rq[...] = sum3(dot(q3, res[...], NT)).reshape(NC, HALF, ROWS)
    r_ex = go(copy(rq.at[1 - c], rqin, esend.at[2], erecv.at[1], sibling))
    wqr[y] = wqh[:, pl.ds(pl.multiple_of(y * PAIR, PAIR), PAIR)]
    for d in range(1, NY):
        i = other(y, d, NY)
        copy(wqr.at[i], wqr.at[i], wsend.at[d], wrecv.at[i], sibling).wait_recv()
    w_tok = wqr[0]
    for i in range(1, NY):
        w_tok = w_tok + wqr[i]
    sib_slot = gbuf.at[y * NC + (1 - c)]
    copy(sib_slot, sib_slot, esend.at[1], cown, sibling).wait_recv()
    pair = gbuf[pl.ds(y * NC, NC)].reshape(PAIR, ROWS)
    p_tok = sum3(dot(split3(w_tok * SCALE), pair, NN))
    r_ex.wait_recv()
    ph[...] = p_tok + (rq[c] + rqin[...])

    for d in range(1, NX):
        i = other(x, d, NX)
        go(copy(ph.at[:, pl.ds(pl.multiple_of(i * XL, 128), XL)], xr.at[x], xsend.at[d], xrecv.at[x], at_x(i)))
    ring_step(1, 0)
    ring_step(1, 1)
    xr[x] = ph[:, pl.ds(pl.multiple_of(x * XL, 128), XL)]
    for d in range(1, NX):
        i = other(x, d, NX)
        copy(xr.at[i], xr.at[i], xsend.at[d], xrecv.at[i], sibling).wait_recv()
    total = xr[0]
    for i in range(1, NX):
        total = total + xr[i]
    for i in range(NZ):
        zs[i] = total[ZR * i : ZR * (i + 1)]
    for d in range(1, NZ):
        i = other(z, d, NZ)
        go(copy(zs.at[i], zr.at[z], zsend.at[d], zrecv.at[z], at_z(i)))
    ring_step(2, 0)
    zr[z] = zs[z]
    for d in range(1, NZ):
        i = other(z, d, NZ)
        copy(zr.at[i], zr.at[i], zsend.at[d], zrecv.at[i], sibling).wait_recv()
    total = zr[0]
    for i in range(1, NZ):
        total = total + zr[i]
    yr[y] = total
    for d in range(1, NY):
        i = other(y, d, NY)
        go(copy(yr.at[y], yr.at[y], ysend.at[d], yrecv.at[y], at_y(i)))
    ring_step(2, 1)
    for d in range(1, NY):
        i = other(y, d, NY)
        copy(yr.at[i], yr.at[i], ysend.at[d], yrecv.at[i], sibling).wait_recv()
    total = yr[0]
    for i in range(1, NY):
        total = total + yr[i]
    zg[z] = total
    for d in range(1, NZ):
        i = other(z, d, NZ)
        go(copy(zg.at[z], zg.at[z], zgsend.at[d], zgrecv.at[z], at_z(i)))
    ring_step(3, 0)
    ring_step(3, 1)
    for d in range(1, NZ):
        i = other(z, d, NZ)
        copy(zg.at[i], zg.at[i], zgsend.at[d], zgrecv.at[i], sibling).wait_recv()
    for i in range(NZ):
        pa[ZR * i : ZR * (i + 1), :] = zg[i]
    mine = pl.ds(pl.multiple_of(x * XL, 128), XL)
    for d in range(1, NX):
        i = other(x, d, NX)
        go(copy(pa, pt.at[c, :, mine], xgsend.at[d], xgrecv.at[x], at_x(i)))
    pt[c, :, mine] = pa[...]
    for d in range(1, NX):
        i = other(x, d, NX)
        theirs = pt.at[c, :, pl.ds(pl.multiple_of(i * XL, 128), XL)]
        copy(theirs, theirs, xgsend.at[d], xgrecv.at[i], sibling).wait_recv()
    go(copy(pt.at[c], pt.at[c], esend.at[3], erecv.at[2], sibling))
    ring_step(4, 0)
    ring_step(4, 1)
    for h in range(1, NY // 2 + 1):
        for s in range(2):
            for up in (True, False):
                if h == NY // 2 and (s == 0) != up:
                    continue
                u = 0 if up else 1
                slot = lax.rem(y + (NY - h if up else h), NY) * NC + (1 - c)
                part = gbuf.at[slot, pl.ds(s * SUB, SUB)]
                copy(part, part, csend.at[u, h - 1, s], crecv.at[u, h - 1, s], sibling).wait_recv()
    copy(pt.at[1 - c], pt.at[1 - c], esend.at[3], erecv.at[2], sibling).wait_recv()

    p = pt[...].reshape(RANK, ROWS)
    p3 = split3(p)
    tokens = gbuf[...].reshape(TOK, ROWS)
    u3 = split3(sum3(dot(p3, tokens, NT)) * SCALE)
    q_part = sum3(dot(u3, wbuf[...], NN)) + sum3(dot(p3, res[...], NN))
    qb[...] = jnp.concatenate([q_part, jnp.zeros((RANK, QL - COLS), F32)], axis=1)
    for d in range(1, NX):
        i = other(x, d, NX)
        go(copy(qb.at[pl.ds(pl.multiple_of(i * QR, QR), QR)], qxr.at[x], qxsend.at[d], qxrecv.at[x], at_x(i)))

    step_cols = 512

    def grad(i, carry):
        at = pl.ds(pl.multiple_of(i * step_cols, step_cols), step_cols)
        g = dot(gbuf[:, :, at].reshape(TOK, step_cols), wbuf[...], TN)
        merged[at, :] = g * SCALE + res[at, :].astype(F32)
        return carry

    lax.fori_loop(0, ROWS // step_cols, grad, 0)
    store = pltpu.make_async_copy(merged, merged_hbm, lsem.at[5])
    store.start()
    qxr[x] = qb[pl.ds(pl.multiple_of(x * QR, QR), QR), :]
    for d in range(1, NX):
        i = other(x, d, NX)
        copy(qxr.at[i], qxr.at[i], qxsend.at[d], qxrecv.at[i], sibling).wait_recv()
    total = qxr[0]
    for i in range(1, NX):
        total = total + qxr[i]
    qzr[z] = total
    for d in range(1, NZ):
        i = other(z, d, NZ)
        go(copy(qzr.at[z], qzr.at[z], qzsend.at[d], qzrecv.at[z], at_z(i)))
    inv = inverse_factor(dot_exact(p, p, NT))
    phat_ref[...] = dot_exact(inv, p, NN)
    for d in range(1, NZ):
        i = other(z, d, NZ)
        copy(qzr.at[i], qzr.at[i], qzsend.at[d], qzrecv.at[i], sibling).wait_recv()
    total = qzr[0]
    for i in range(1, NZ):
        total = total + qzr[i]
    qt[x] = total
    for d in range(1, NX):
        i = other(x, d, NX)
        go(copy(qt.at[x], qt.at[x], qgsend.at[d], qgrecv.at[x], at_x(i)))
    for d in range(1, NX):
        i = other(x, d, NX)
        copy(qt.at[i], qt.at[i], qgsend.at[d], qgrecv.at[i], sibling).wait_recv()
    qnext_ref[...] = dot_exact(inv, qt[...].reshape(RANK, QL), NN)
    store.wait()
    for cp in pending:
        cp.wait_send()


def chain(inputs, out_grads, counts, residual, q_start):
    dma = pltpu.SemaphoreType.DMA
    vmem = pltpu.VMEM
    return pl.pallas_call(
        chain_kernel,
        out_shape=(
            jax.ShapeDtypeStruct((ROWS, COLS), F32),
            jax.ShapeDtypeStruct((RANK, ROWS), F32),
            jax.ShapeDtypeStruct((RANK, QL), F32),
        ),
        in_specs=[pl.BlockSpec(memory_space=pl.ANY)] * 5,
        out_specs=(
            pl.BlockSpec(memory_space=pl.ANY),
            pl.BlockSpec(memory_space=pltpu.VMEM),
            pl.BlockSpec(memory_space=pltpu.VMEM),
        ),
        scratch_shapes=[
            vmem((NY * NC, BLOCK, ROWS), BF16),
            vmem((TOK, COLS), BF16),
            vmem((1, TOK), jnp.int32),
            vmem((ROWS, COLS), BF16),
            vmem((COLS, RANK), F32),
            vmem((TOK, COLS), BF16),
            vmem((ROWS, COLS), F32),
            vmem((NC, HALF, TOK), F32),
            vmem((HALF, TOK), F32),
            vmem((HALF, TOK), F32),
            vmem((NY, HALF, PAIR), F32),
            vmem((NC, HALF, ROWS), F32),
            vmem((HALF, ROWS), F32),
            vmem((HALF, ROWS), F32),
            vmem((NX, HALF, XL), F32),
            vmem((HALF, XL), F32),
            vmem((NZ, ZR, XL), F32),
            vmem((NZ, ZR, XL), F32),
            vmem((NY, ZR, XL), F32),
            vmem((NZ, ZR, XL), F32),
            vmem((HALF, XL), F32),
            vmem((NC, HALF, ROWS), F32),
            vmem((RANK, QL), F32),
            vmem((NX, QR, QL), F32),
            vmem((NZ, QR, QL), F32),
            vmem((NX, QR, QL), F32),
            dma((6,)),
            dma((2, 4, 2)), dma((2, 4, 2)),
            dma((2, 4, 2)), dma((2, 4, 2)),
            dma,
            dma((4,)), dma((3,)),
            dma((NY,)), dma((NY,)),
            dma((NX,)), dma((NX,)),
            dma((NZ,)), dma((NZ,)),
            dma((NY,)), dma((NY,)),
            dma((NZ,)), dma((NZ,)),
            dma((NX,)), dma((NX,)),
            dma((NX,)), dma((NX,)),
            dma((NZ,)), dma((NZ,)),
            dma((NX,)), dma((NX,)),
        ],
        compiler_params=pltpu.CompilerParams(
            collective_id=0, has_side_effects=True, vmem_limit_bytes=48 << 20
        ),
        name="chain",
    )(inputs, out_grads, counts, residual, q_start)


FINAL_ROWS = 512


def final_kernel(merged_ref, phat_ref, qnext_ref, update_ref, res_ref, q_ref, approx):
    i = pl.program_id(0)

    def high_low(v):
        high = v.astype(BF16)
        return high, (v - high.astype(F32)).astype(BF16)

    p_high, p_low = high_low(phat_ref[...])
    q_high, q_low = high_low(qnext_ref[...][:, :COLS])
    block = dot(
        jnp.concatenate([p_high, p_high, p_low], axis=0),
        jnp.concatenate([q_high, q_low, q_high], axis=0),
        TN,
    )
    res_ref[...] = (merged_ref[...] - block * (1.0 / (NX * NZ))).astype(BF16)
    approx[pl.ds(pl.multiple_of(i * FINAL_ROWS, FINAL_ROWS), FINAL_ROWS), :] = block

    @pl.when(i == 0)
    def _():
        q_ref[...] = qnext_ref[...].T[:COLS]

    @pl.when(i == pl.num_programs(0) - 1)
    def _():
        n = ROWS // (NX * NZ)
        start = pl.multiple_of(lax.axis_index("dp") * n, 8)
        update_ref[...] = approx[pl.ds(start, n), :].astype(BF16)


def final(merged, phat, qnext):
    n = ROWS // (NX * NZ)
    return pl.pallas_call(
        final_kernel,
        grid=(ROWS // FINAL_ROWS,),
        out_shape=(
            jax.ShapeDtypeStruct((n, COLS), BF16),
            jax.ShapeDtypeStruct((ROWS, COLS), BF16),
            jax.ShapeDtypeStruct((COLS, RANK), F32),
        ),
        in_specs=[
            pl.BlockSpec((FINAL_ROWS, COLS), lambda i: (i, 0)),
            pl.BlockSpec((RANK, FINAL_ROWS), lambda i: (0, i)),
            pl.BlockSpec((RANK, QL), lambda i: (0, 0)),
        ],
        out_specs=(
            pl.BlockSpec((n, COLS), lambda i: (0, 0)),
            pl.BlockSpec((FINAL_ROWS, COLS), lambda i: (i, 0)),
            pl.BlockSpec((COLS, RANK), lambda i: (0, 0)),
        ),
        scratch_shapes=[pltpu.VMEM((ROWS, COLS), F32)],
        compiler_params=pltpu.CompilerParams(vmem_limit_bytes=32 << 20),
        name="final",
    )(merged, phat, qnext)


def local(inputs, out_grads, counts, residual, q_start):
    merged, phat, qnext = chain(inputs[0], out_grads[0], counts, residual[0], q_start)
    update, residual_next, q_next = final(merged, phat, qnext)
    return update, residual_next[None], q_next


def solution(mesh):
    return jax.shard_map(
        local,
        mesh=mesh,
        in_specs=(
            P("dp", "mp", None),
            P("dp", None, "mp"),
            P("dp", None),
            P("dp", None, "mp"),
            P("mp", None),
        ),
        out_specs=(P("dp", "mp"), P("dp", None, "mp"), P("mp", None)),
        check_vma=False,
    )
```

time: 504 us -> 81.9 us (0.16)
  the two profiles are of different devices: /device:TPU:32 before, /device:TPU:1 now
where the time goes in v1:
time: 81.9 us; the launch traced here: 81.6 us
  Pallas kernels  68.8 us (84%)
  local copies, waits for them, and re-layouts  12.1 us (15%)
    pallas_call x1, Pallas kernels, chain(): pl.pallas_call(chain_kernel, out_shape=(jax.ShapeDtypeStruct((ROWS, COLS)...  66.5 us
    unnamed x11, local copies, waits for them, and re-layouts  12.1 us
    pallas_call x1, Pallas kernels, final(): pl.pallas_call(final_kernel, grid=(ROWS // FINAL_ROWS,), out_shape=(jax.S...  2.28 us

profile of v1, /device:TPU:1, one launch (start us, length us, event | category | flops | bytes accessed | tf_op | source)
XLA Modules:
  0.0 81.6 jit_solution(9802221196659900773)
XLA Ops:
  0.6 0.9 %copy.10.q_hbm = f32[320,32]{1,0:T(8,128)S(1)} copy(f32[320,32]{0,1:T(8,128)} %param.9) | data formatting | bytes 81920 | tf_op args[4]
  1.5 1.4 %copy.8 = bf16[1,1024,320]{2,1,0:T(8,128)(2,1)S(1)} copy(bf16[1,1024,320]{1,2,0:T(8,128)(2,1)} %param.6) | data formatting | bytes 1310720 | tf_op args[1]
  3.0 0.0 copy-start.1
  3.0 0.0 copy-start.2
  3.0 3.7 %copy.9 = bf16[1,2560,320]{2,1,0:T(8,128)(2,1)S(1)} copy(bf16[1,2560,320]{1,2,0:T(8,128)(2,1)} %param.8) | data formatting | bytes 3276800 | tf_op args[3]
  6.7 0.0 copy-done.1
  6.7 0.0 copy-done.2
  6.7 66.5 %chain.1 = (f32[2560,320]{1,0:T(8,128)}, f32[32,2560]{1,0:T(8,128)S(1)}, f32[32,384]{1,0:T(8,128)S(1)}) custom-call(bf16[64,2560]{1,0:T(8,128)(2,1)S(1)} %bitcast.7, bf16[1024,320]{1,0:T(8,128)(2,1)S(1)} %bitcast.5, s32[1,1024]{1,0:T(1,128)S(1)} %copy-done.2, bf16[2560,320]{1,0:T(8,128)(2,1)S(1)} %bitcast.4, f32[320,32]{1,0:T(8,128)S(1)} %copy.10.q_hbm), custom_call_target="tpu_custom_call" | custom-call | tf_op jit(solution)/shard_map/chain/pallas_call | solution.py:311
  73.2 0.0 copy-start
  73.2 2.1 %copy-done = f32[2560,320]{1,0:T(8,128)S(1)} copy-done((f32[2560,320]{1,0:T(8,128)S(1)}, f32[2560,320]{1,0:T(8,128)}, u32[]{:S(2)}) %copy-start) | copy-done | bytes 3276824
  75.3 2.3 %final.1 = (bf16[80,320]{1,0:T(8,128)(2,1)}, bf16[2560,320]{1,0:T(8,128)(2,1)S(1)}, f32[320,32]{1,0:T(8,128)S(1)}) custom-call(f32[2560,320]{1,0:T(8,128)S(1)} %copy-done, f32[32,2560]{1,0:T(8,128)S(1)} %get-tuple-element.10.phat_ref, f32[32,384]{1,0:T(8,128)S(1)} %get-tuple-element.11.qnext_ref), custom_call_target="tpu_custom_call" | custom-call | tf_op jit(solution)/shard_map/final/pallas_call | solution.py:406
  77.6 3.2 %copy.11 = bf16[1,2560,320]{1,2,0:T(8,128)(2,1)} copy(bf16[1,2560,320]{2,1,0:T(8,128)(2,1)S(1)} %bitcast.6) | data formatting | bytes 3276800
  80.8 0.7 copy.12
Async XLA Ops:
  3.0 3.7 %copy-start.1 = (bf16[1,64,2560]{2,1,0:T(8,128)(2,1)S(1)}, bf16[1,64,2560]{2,1,0:T(8,128)(2,1)}, u32[]{:S(2)}) copy-start(bf16[1,64,2560]{2,1,0:T(8,128)(2,1)} %param.5) | copy-start | bytes 983044
  3.0 3.7 %copy-start.2 = (s32[1,1024]{1,0:T(1,128)S(1)}, s32[1,1024]{1,0:T(1,128)}, u32[]{:S(2)}) copy-start(s32[1,1024]{1,0:T(1,128)} %cnt_hbm.1) | copy-start | bytes 12292
  73.2 2.1 %copy-start = (f32[2560,320]{1,0:T(8,128)S(1)}, f32[2560,320]{1,0:T(8,128)}, u32[]{:S(2)}) copy-start(f32[2560,320]{1,0:T(8,128)} %get-tuple-element.9.merged_ref) | copy-start | bytes 9830404

commit v2 on v1

v2 whole, which is shorter than its diff:
```python
import functools

import jax
import jax.numpy as jnp
from jax import lax
from jax.experimental import pallas as pl
from jax.experimental.pallas import tpu as pltpu
from jax.sharding import PartitionSpec as P

MESH = pl.DeviceIdType.MESH
F32, BF16 = jnp.float32, jnp.bfloat16
NX, NY, NZ, NC = 4, 8, 8, 2
ROWS, COLS, RANK, TOK = 2560, 320, 32, 1024
HALF = RANK // NC
BLOCK = TOK // (NY * NC)
PAIR = BLOCK * NC
XL = ROWS // NX
ZR = HALF // NZ
QR = RANK // NX
QL = 384
SUB = BLOCK // 2
GRAD_LANES = 640


def far_first(*sizes):
    offsets = [()]
    for n in sizes:
        offsets = [o + (d,) for o in offsets for d in range(n)]
    return sorted(offsets, key=lambda o: -sum(min(d, n - d) for d, n in zip(o, sizes)))[:-1]


FAR_X, FAR_Y, FAR_Z = ([d for (d,) in far_first(n)] for n in (NX, NY, NZ))
FAR_PLANE = far_first(NX, NZ)
SCALE = 1.0 / 32.0
DIVISOR = 8.0
NT = (((1,), (1,)), ((), ()))
NN = (((1,), (0,)), ((), ()))
TN = (((0,), (0,)), ((), ()))


def dot(a, b, dims):
    return lax.dot_general(a, b, dims, preferred_element_type=F32)


def dot_exact(a, b, dims):
    return lax.dot_general(a, b, dims, precision=lax.Precision.HIGHEST, preferred_element_type=F32)


def split3(v):
    high = v.astype(BF16)
    rest = v - high.astype(F32)
    mid = rest.astype(BF16)
    low = (rest - mid.astype(F32)).astype(BF16)
    return jnp.concatenate([high, mid, low], axis=0)


def sum3(v):
    n = v.shape[0] // 3
    return v[:n] + (v[n : 2 * n] + v[2 * n :])


def inverse_factor(gram):
    rows = lax.broadcasted_iota(jnp.int32, (RANK, 128), 0)
    lanes = lax.broadcasted_iota(jnp.int32, (RANK, 128), 1)
    eye = jnp.where(lanes == rows + RANK, 1.0, 0.0)
    work = jnp.concatenate([gram, jnp.zeros((RANK, 128 - RANK), F32)], axis=1) + eye

    pivots = jnp.ones((RANK, 128), F32)
    for j in range(RANK):
        col = jnp.broadcast_to(work[:, j : j + 1], (RANK, 128))
        pivot = col[j : j + 1]
        pivots = jnp.where(rows == j, pivot, pivots)
        work = jnp.where(rows > j, work - col * (work[j : j + 1] / pivot), work)
    return (work / jnp.sqrt(pivots))[:, RANK : 2 * RANK]


def chain_kernel(
    inp_hbm, og_hbm, cnt_hbm, res_hbm, q_hbm,
    merged, phat_ref, qnext_ref,
    gbuf, og, cnt, res, q, wbuf,
    wq, wqin, wqh, wqr, rq, rqin, ph, ps, pr, yr, pg, pt,
    qb, qxr, qzr, qt,
    lsem, gsend, grecv, csend, crecv, cown, esend, erecv,
    wsend, wrecv, psend, precv, ysend, yrecv, pgsend, pgrecv, plane, qxsend, qxrecv, qzsend, qzrecv, qgsend, qgrecv,
):
    dp, mp = lax.axis_index("dp"), lax.axis_index("mp")
    x, z = dp // NZ, lax.rem(dp, NZ)
    y, c = mp // NC, lax.rem(mp, NC)

    def at_x(i):
        return (i * NZ + z, mp)

    def at_z(i):
        return (x * NZ + i, mp)

    def at_y(i):
        return (dp, i * NC + c)

    sibling = (dp, y * NC + (1 - c))

    def other(i, d, n):
        return lax.rem(i + d, n)

    def at_dp(i):
        return (i, mp)

    def offset(dx, dz):
        return other(x, dx, NX) * NZ + other(z, dz, NZ)

    def copy(src, dst, s, r, to):
        return pltpu.make_async_remote_copy(src, dst, s, r, device_id=to, device_id_type=MESH)

    loads = [
        pltpu.make_async_copy(og_hbm, og, lsem.at[0]),
        pltpu.make_async_copy(cnt_hbm, cnt, lsem.at[1]),
        pltpu.make_async_copy(q_hbm, q, lsem.at[2]),
        pltpu.make_async_copy(inp_hbm, gbuf.at[mp], lsem.at[3]),
        pltpu.make_async_copy(res_hbm, res, lsem.at[4]),
    ]
    for load in loads:
        load.start()

    barrier = pltpu.get_barrier_semaphore()
    peers = [sibling]
    peers += [at_x(other(x, d, NX)) for d in range(1, NX)]
    peers += [at_z(other(z, d, NZ)) for d in range(1, NZ)]
    peers += [at_y(other(y, d, NY)) for d in range(1, NY)]
    for peer in peers:
        pl.semaphore_signal(barrier, inc=1, device_id=peer, device_id_type=MESH)

    loads[0].wait()
    loads[1].wait()
    loads[2].wait()
    weight = cnt[...].astype(F32) * (SCALE / DIVISOR)
    wbuf[...] = (og[...].astype(F32) * weight).astype(BF16)
    q3 = split3(q[...])
    wq[...] = sum3(dot(q3, wbuf[...], NN)).reshape(NC, HALF, TOK)
    pl.semaphore_wait(barrier, len(peers))
    for d in FAR_Z:
        pl.semaphore_signal(plane, inc=1, device_id=at_z(other(z, d, NZ)), device_id_type=MESH)

    pending = []

    def go(cp):
        cp.start()
        pending.append(cp)
        return cp

    w_ex = go(copy(wq.at[1 - c], wqin, esend.at[0], erecv.at[0], sibling))
    loads[3].wait()
    own_ex = go(copy(gbuf.at[mp], gbuf.at[mp], esend.at[1], cown, sibling))
    w_ex.wait_recv()
    wqh[...] = wq[c] + wqin[...]
    for d in FAR_Y:
        i = other(y, d, NY)
        go(copy(wqh.at[:, pl.ds(pl.multiple_of(i * PAIR, PAIR), PAIR)], wqr.at[y], wsend.at[d], wrecv.at[y], at_y(i)))

    def ring_block(up, h):
        return lax.rem(y + (NY - h if up else h), NY) * NC + c

    def ring_send(up, h, s):
        part = gbuf.at[ring_block(up, h), pl.ds(s * SUB, SUB)]
        to = at_y(other(y, 1 if up else NY - 1, NY))
        u = 0 if up else 1
        go(copy(part, part, gsend.at[u, h, s], grecv.at[u, h, s], to))

    def ring_recv(up, h, s):
        part = gbuf.at[ring_block(up, h), pl.ds(s * SUB, SUB)]
        u = 0 if up else 1
        copy(part, part, gsend.at[u, h - 1, s], grecv.at[u, h - 1, s], sibling).wait_recv()
        go(copy(part, part, csend.at[u, h - 1, s], crecv.at[u, h - 1, s], sibling))

    def ring_step(h, s):
        for up in (True, False):
            if h == NY // 2 and (s == 0) != up:
                continue
            ring_recv(up, h, s)
            if h < NY // 2 - 1 or (h == NY // 2 - 1 and (s == 0) == up):
                ring_send(up, h, s)

    def ring_sibling(h):
        for s in range(2):
            for up in (True, False):
                if h == NY // 2 and (s == 0) != up:
                    continue
                u = 0 if up else 1
                slot = lax.rem(y + (NY - h if up else h), NY) * NC + (1 - c)
                part = gbuf.at[slot, pl.ds(s * SUB, SUB)]
                copy(part, part, csend.at[u, h - 1, s], crecv.at[u, h - 1, s], sibling).wait_recv()

    def grad(up, down, first=False):
        up, down = lax.rem(y + NY - up, NY), lax.rem(y + down, NY)

        def lanes(i):
            return pl.ds(pl.multiple_of(i * PAIR, PAIR), PAIR)

        w = jnp.concatenate([wbuf[:, lanes(up)], wbuf[:, lanes(down)]], axis=1)

        def step(i, carry):
            at = pl.ds(pl.multiple_of(i * GRAD_LANES, GRAD_LANES), GRAD_LANES)
            t = jnp.concatenate(
                [gbuf[pl.ds(k * NC, NC), :, at].reshape(PAIR, GRAD_LANES) for k in (up, down)], axis=0
            )
            base = res[:, at].astype(F32) if first else merged[:, at]
            merged[:, at] = base + dot(w, t, NN)
            return carry

        lax.fori_loop(0, ROWS // GRAD_LANES, step, 0)

    for s in range(2):
        ring_send(True, 0, s)
        ring_send(False, 0, s)

    loads[4].wait()
    rq[...] = sum3(dot(q3, res[...], NN)).reshape(NC, HALF, ROWS)
    r_ex = go(copy(rq.at[1 - c], rqin, esend.at[2], erecv.at[1], sibling))
    wqr[y] = wqh[:, pl.ds(pl.multiple_of(y * PAIR, PAIR), PAIR)]
    for d in range(1, NY):
        i = other(y, d, NY)
        copy(wqr.at[i], wqr.at[i], wsend.at[d], wrecv.at[i], sibling).wait_recv()
    w_tok = wqr[0]
    for i in range(1, NY):
        w_tok = w_tok + wqr[i]
    sib_slot = gbuf.at[y * NC + (1 - c)]
    copy(sib_slot, sib_slot, esend.at[1], cown, sibling).wait_recv()
    pair = gbuf[pl.ds(y * NC, NC)].reshape(PAIR, ROWS)
    p_tok = sum3(dot(split3(w_tok), pair, NN))
    r_ex.wait_recv()
    ph[...] = p_tok + (rq[c] + rqin[...])

    for i in range(NX):
        for k in range(NZ):
            ps[i * NZ + k] = ph[ZR * k : ZR * (k + 1), XL * i : XL * (i + 1)]
    pl.semaphore_wait(plane, NZ - 1)
    for n, (dx, dz) in enumerate(FAR_PLANE):
        i = offset(dx, dz)
        go(copy(ps.at[i], pr.at[dp], psend.at[n], precv.at[dp], at_dp(i)))
    ring_step(1, 0)
    ring_step(1, 1)
    pr[dp] = ps[dp]
    for dx, dz in FAR_PLANE[::-1]:
        i = offset(dx, dz)
        copy(pr.at[i], pr.at[i], psend.at[0], precv.at[i], sibling).wait_recv()
    yr[y] = jnp.sum(pr[...], axis=0)
    for d in FAR_Y:
        i = other(y, d, NY)
        go(copy(yr.at[y], yr.at[y], ysend.at[d], yrecv.at[y], at_y(i)))
    ring_step(2, 0)
    ring_step(2, 1)
    ring_sibling(1)
    grad(1, 1, first=True)
    for d in range(1, NY):
        i = other(y, d, NY)
        copy(yr.at[i], yr.at[i], ysend.at[d], yrecv.at[i], sibling).wait_recv()
    pg[dp] = jnp.sum(yr[...], axis=0)
    for n, (dx, dz) in enumerate(FAR_PLANE):
        i = offset(dx, dz)
        go(copy(pg.at[dp], pg.at[dp], pgsend.at[n], pgrecv.at[dp], at_dp(i)))
    ring_step(3, 0)
    ring_step(3, 1)
    ring_sibling(2)
    grad(2, 2)
    for dx, dz in FAR_PLANE[::-1]:
        i = offset(dx, dz)
        copy(pg.at[i], pg.at[i], pgsend.at[0], pgrecv.at[i], sibling).wait_recv()
    for i in range(NX):
        for k in range(NZ):
            pt[c, ZR * k : ZR * (k + 1), XL * i : XL * (i + 1)] = pg[i * NZ + k]
    go(copy(pt.at[c], pt.at[c], esend.at[3], erecv.at[2], sibling))
    ring_step(4, 0)
    ring_step(4, 1)
    ring_sibling(3)
    ring_sibling(4)
    copy(pt.at[1 - c], pt.at[1 - c], esend.at[3], erecv.at[2], sibling).wait_recv()

    p = pt[...].reshape(RANK, ROWS)
    p3 = split3(p)
    tokens = gbuf[...].reshape(TOK, ROWS)
    u3 = split3(sum3(dot(p3, tokens, NT)))
    q_part = sum3(dot(u3, wbuf[...], NT)) + sum3(dot(p3, res[...], NT))
    qb[...] = jnp.concatenate([q_part, jnp.zeros((RANK, QL - COLS), F32)], axis=1)
    for d in FAR_X:
        i = other(x, d, NX)
        go(copy(qb.at[pl.ds(pl.multiple_of(i * QR, QR), QR)], qxr.at[x], qxsend.at[d], qxrecv.at[x], at_x(i)))

    grad(3, 3)
    grad(0, 4)
    qxr[x] = qb[pl.ds(pl.multiple_of(x * QR, QR), QR), :]
    for d in range(1, NX):
        i = other(x, d, NX)
        copy(qxr.at[i], qxr.at[i], qxsend.at[d], qxrecv.at[i], sibling).wait_recv()
    total = qxr[0]
    for i in range(1, NX):
        total = total + qxr[i]
    qzr[z] = total
    for d in FAR_Z:
        i = other(z, d, NZ)
        go(copy(qzr.at[z], qzr.at[z], qzsend.at[d], qzrecv.at[z], at_z(i)))
    inv = inverse_factor(dot_exact(p, p, NT))
    for d in range(1, NZ):
        i = other(z, d, NZ)
        copy(qzr.at[i], qzr.at[i], qzsend.at[d], qzrecv.at[i], sibling).wait_recv()
    total = qzr[0]
    for i in range(1, NZ):
        total = total + qzr[i]
    qt[x] = total
    for d in FAR_X:
        i = other(x, d, NX)
        go(copy(qt.at[x], qt.at[x], qgsend.at[d], qgrecv.at[x], at_x(i)))
    phat_ref[...] = dot_exact(inv, p, NN)
    for d in range(1, NX):
        i = other(x, d, NX)
        copy(qt.at[i], qt.at[i], qgsend.at[d], qgrecv.at[i], sibling).wait_recv()
    qnext_ref[...] = dot_exact(inv, qt[...].reshape(RANK, QL), NN)
    for cp in pending:
        cp.wait_send()


def chain(inputs, out_grads, counts, residual, q_start):
    dma = pltpu.SemaphoreType.DMA
    vmem = pltpu.VMEM
    return pl.pallas_call(
        chain_kernel,
        out_shape=(
            vmem((COLS, ROWS), F32),
            vmem((RANK, ROWS), F32),
            vmem((RANK, QL), F32),
        ),
        in_specs=[pl.BlockSpec(memory_space=pl.ANY)] * 5,
        out_specs=(
            pl.BlockSpec(memory_space=pltpu.VMEM),
            pl.BlockSpec(memory_space=pltpu.VMEM),
            pl.BlockSpec(memory_space=pltpu.VMEM),
        ),
        scratch_shapes=[
            vmem((NY * NC, BLOCK, ROWS), BF16),
            vmem((COLS, TOK), BF16),
            vmem((1, TOK), jnp.int32),
            vmem((COLS, ROWS), BF16),
            vmem((RANK, COLS), F32),
            vmem((COLS, TOK), BF16),
            vmem((NC, HALF, TOK), F32),
            vmem((HALF, TOK), F32),
            vmem((HALF, TOK), F32),
            vmem((NY, HALF, PAIR), F32),
            vmem((NC, HALF, ROWS), F32),
            vmem((HALF, ROWS), F32),
            vmem((HALF, ROWS), F32),
            vmem((NX * NZ, ZR, XL), F32),
            vmem((NX * NZ, ZR, XL), F32),
            vmem((NY, ZR, XL), F32),
            vmem((NX * NZ, ZR, XL), F32),
            vmem((NC, HALF, ROWS), F32),
            vmem((RANK, QL), F32),
            vmem((NX, QR, QL), F32),
            vmem((NZ, QR, QL), F32),
            vmem((NX, QR, QL), F32),
            dma((5,)),
            dma((2, 4, 2)), dma((2, 4, 2)),
            dma((2, 4, 2)), dma((2, 4, 2)),
            dma,
            dma((4,)), dma((3,)),
            dma((NY,)), dma((NY,)),
            dma((NX * NZ,)), dma((NX * NZ,)),
            dma((NY,)), dma((NY,)),
            dma((NX * NZ,)), dma((NX * NZ,)),
            pltpu.SemaphoreType.REGULAR,
            dma((NX,)), dma((NX,)),
            dma((NZ,)), dma((NZ,)),
            dma((NX,)), dma((NX,)),
        ],
        compiler_params=pltpu.CompilerParams(
            collective_id=0, has_side_effects=True, vmem_limit_bytes=40 << 20
        ),
        name="chain",
    )(*(pltpu.with_memory_space_constraint(a, pltpu.HBM) for a in (inputs, out_grads, counts, residual, q_start)))


FINAL_LANES = 640
OWN = ROWS // (NX * NZ)


def final_kernel(
    merged_ref, phat_ref, qnext_ref, update_hbm, res_hbm, q_hbm,
    update, res, q, turned, sems,
):
    def high_low(v):
        high = v.astype(BF16)
        return high, (v - high.astype(F32)).astype(BF16)

    stores = []

    def store(src, dst):
        stores.append(pltpu.make_async_copy(src, dst, sems.at[len(stores)]))
        stores[-1].start()

    q[...] = qnext_ref[:, :COLS]
    store(q, q_hbm)
    high, low = high_low(qnext_ref[...].T)
    q_cols = jnp.concatenate([high, low, high], axis=1)[:COLS]
    for i in range(ROWS // FINAL_LANES):
        at = slice(i * FINAL_LANES, (i + 1) * FINAL_LANES)
        high, low = high_low(phat_ref[:, at])
        block = dot(q_cols, jnp.concatenate([high, high, low], axis=0), NN)
        res[:, at] = (merged_ref[:, at] - block * (1.0 / (NX * NZ))).astype(BF16)
        store(res.at[:, at], res_hbm.at[:, at])
    first = lax.axis_index("dp") * OWN
    base = jnp.minimum(first // 128, ROWS // 128 - 2) * 128
    turned[...] = phat_ref[:, pl.ds(pl.multiple_of(base, 128), 256)].T
    high, low = high_low(turned[pl.ds(pl.multiple_of(first - base, 8), OWN), :])
    update[...] = dot(jnp.concatenate([high, high, low], axis=1), q_cols, NT).astype(BF16)
    store(update, update_hbm)
    for cp in stores:
        cp.wait()


def final(merged, phat, qnext):
    shapes = ((OWN, COLS), BF16), ((COLS, ROWS), BF16), ((RANK, COLS), F32)
    return pl.pallas_call(
        final_kernel,
        out_shape=tuple(jax.ShapeDtypeStruct(*s) for s in shapes),
        in_specs=[pl.BlockSpec(memory_space=pltpu.VMEM)] * 3,
        out_specs=(pl.BlockSpec(memory_space=pl.ANY),) * 3,
        scratch_shapes=[
            *(pltpu.VMEM(*s) for s in shapes),
            pltpu.VMEM((256, RANK), F32),
            pltpu.SemaphoreType.DMA((ROWS // FINAL_LANES + 2,)),
        ],
        compiler_params=pltpu.CompilerParams(vmem_limit_bytes=24 << 20),
        name="final",
    )(*(pltpu.with_memory_space_constraint(a, pltpu.VMEM) for a in (merged, phat, qnext)))


def local(inputs, out_grads, counts, residual, q_start):
    merged, phat, qnext = chain(inputs[0], out_grads[0].T, counts, residual[0].T, q_start.T)
    update, residual_next, q_next = final(merged, phat, qnext)
    return update, residual_next.T[None], q_next.T


def solution(mesh):
    return jax.shard_map(
        local,
        mesh=mesh,
        in_specs=(
            P("dp", "mp", None),
            P("dp", None, "mp"),
            P("dp", None),
            P("dp", None, "mp"),
            P("mp", None),
        ),
        out_specs=(P("dp", "mp"), P("dp", None, "mp"), P("mp", None)),
        check_vma=False,
    )
```

time: 81.9 us -> 70.7 us (0.86)
  local copies, waits for them, and re-layouts: 12.1 us -> 0 us
  Pallas kernels: 68.8 us -> 69.9 us
    unnamed x11 -> x0, local copies, waits for them, and re-layouts: 12.1 us -> none
    pallas_call x2, Pallas kernels: 68.8 us -> 69.9 us  [the longest x1 68.2 us: chain(): pl.pallas_call(chain_kernel, out_shape=(vmem((COLS, ROWS), F32), vmem((RA...]
where the time goes in v2:
time: 70.7 us; the launch traced here: 70.6 us
  Pallas kernels  69.9 us (99%)
    pallas_call x1, Pallas kernels, chain(): pl.pallas_call(chain_kernel, out_shape=(vmem((COLS, ROWS), F32), vmem((RA...  68.2 us
    pallas_call x1, Pallas kernels, final(): pl.pallas_call(final_kernel, out_shape=tuple((jax.ShapeDtypeStruct(*s) fo...  1.79 us

profile of v2, /device:TPU:1, one launch (start us, length us, event | category | flops | bytes accessed | tf_op | source)
XLA Modules:
  0.0 70.6 jit_solution(11812180748804685398)
XLA Ops:
  0.6 68.2 %chain.1 = (f32[320,2560]{1,0:T(8,128)S(1)}, f32[32,2560]{1,0:T(8,128)S(1)}, f32[32,384]{1,0:T(8,128)S(1)}) custom-call(bf16[64,2560]{1,0:T(8,128)(2,1)} %bitcast.14, bf16[320,1024]{1,0:T(8,128)(2,1)} %bitcast.13, s32[1,1024]{1,0:T(1,128)} %cnt_hbm.1, bf16[320,2560]{1,0:T(8,128)(2,1)} %bitcast.12, f32[32,320]{1,0:T(8,128)} %bitcast.15), custom_call_target="tpu_custom_call" | custom-call | tf_op jit(solution)/shard_map/chain/pallas_call | solution.py:322
  68.8 1.8 %final.1 = (bf16[80,320]{1,0:T(8,128)(2,1)}, bf16[320,2560]{1,0:T(8,128)(2,1)}, f32[32,320]{1,0:T(8,128)}) custom-call(f32[320,2560]{1,0:T(8,128)S(1)} %get-tuple-element.9.merged_ref, f32[32,2560]{1,0:T(8,128)S(1)} %get-tuple-element.10.phat_ref, f32[32,384]{1,0:T(8,128)S(1)} %get-tuple-element.11.qnext_ref), custom_call_target="tpu_custom_call" | custom-call | tf_op jit(solution)/shard_map/final/pallas_call | solution.py:419

commit v3 on v2

--- a/solution.py
+++ b/solution.py
@@ -31,6 +31,7 @@
 
 FAR_X, FAR_Y, FAR_Z = ([d for (d,) in far_first(n)] for n in (NX, NY, NZ))
 FAR_PLANE = far_first(NX, NZ)
+FAR_U = (4, 3, 5)
 SCALE = 1.0 / 32.0
 DIVISOR = 8.0
 NT = (((1,), (1,)), ((), ()))
@@ -79,9 +80,9 @@
     merged, phat_ref, qnext_ref,
     gbuf, og, cnt, res, q, wbuf,
     wq, wqin, wqh, wqr, rq, rqin, ph, ps, pr, yr, pg, pt,
-    qb, qxr, qzr, qt,
+    qb, qxr, qzr, qt, inv, ubuf,
     lsem, gsend, grecv, csend, crecv, cown, esend, erecv,
-    wsend, wrecv, psend, precv, ysend, yrecv, pgsend, pgrecv, plane, qxsend, qxrecv, qzsend, qzrecv, qgsend, qgrecv,
+    wsend, wrecv, psend, precv, ysend, yrecv, pgsend, pgrecv, plane, qxsend, qxrecv, qzsend, qzrecv, qgsend, qgrecv, usend, urecv,
 ):
     dp, mp = lax.axis_index("dp"), lax.axis_index("mp")
     x, z = dp // NZ, lax.rem(dp, NZ)
@@ -146,15 +147,6 @@
         pending.append(cp)
         return cp
 
-    w_ex = go(copy(wq.at[1 - c], wqin, esend.at[0], erecv.at[0], sibling))
-    loads[3].wait()
-    own_ex = go(copy(gbuf.at[mp], gbuf.at[mp], esend.at[1], cown, sibling))
-    w_ex.wait_recv()
-    wqh[...] = wq[c] + wqin[...]
-    for d in FAR_Y:
-        i = other(y, d, NY)
-        go(copy(wqh.at[:, pl.ds(pl.multiple_of(i * PAIR, PAIR), PAIR)], wqr.at[y], wsend.at[d], wrecv.at[y], at_y(i)))
-
     def ring_block(up, h):
         return lax.rem(y + (NY - h if up else h), NY) * NC + c
 
@@ -170,12 +162,14 @@
         copy(part, part, gsend.at[u, h - 1, s], grecv.at[u, h - 1, s], sibling).wait_recv()
         go(copy(part, part, csend.at[u, h - 1, s], crecv.at[u, h - 1, s], sibling))
 
-    def ring_step(h, s):
+    def ring_in(h, s):
         for up in (True, False):
-            if h == NY // 2 and (s == 0) != up:
-                continue
-            ring_recv(up, h, s)
-            if h < NY // 2 - 1 or (h == NY // 2 - 1 and (s == 0) == up):
+            if h < NY // 2 or (s == 0) == up:
+                ring_recv(up, h, s)
+
+    def ring_out(h, s):
+        for up in (True, False):
+            if h < NY // 2 - 1 or (s == 0) == up:
                 ring_send(up, h, s)
 
     def ring_sibling(h):
@@ -188,29 +182,33 @@
                 part = gbuf.at[slot, pl.ds(s * SUB, SUB)]
                 copy(part, part, csend.at[u, h - 1, s], crecv.at[u, h - 1, s], sibling).wait_recv()
 
-    def grad(up, down, first=False):
-        up, down = lax.rem(y + NY - up, NY), lax.rem(y + down, NY)
+    def grad(ups, downs):
+        chips = [lax.rem(y + NY - h, NY) for h in ups] + [lax.rem(y + h, NY) for h in downs]
 
         def lanes(i):
             return pl.ds(pl.multiple_of(i * PAIR, PAIR), PAIR)
 
-        w = jnp.concatenate([wbuf[:, lanes(up)], wbuf[:, lanes(down)]], axis=1)
+        w = jnp.concatenate([wbuf[:, lanes(k)] for k in chips], axis=1)
 
         def step(i, carry):
             at = pl.ds(pl.multiple_of(i * GRAD_LANES, GRAD_LANES), GRAD_LANES)
-            t = jnp.concatenate(
-                [gbuf[pl.ds(k * NC, NC), :, at].reshape(PAIR, GRAD_LANES) for k in (up, down)], axis=0
-            )
-            base = res[:, at].astype(F32) if first else merged[:, at]
-            merged[:, at] = base + dot(w, t, NN)
+            t = [gbuf[pl.ds(k * NC, NC), :, at].reshape(PAIR, GRAD_LANES) for k in chips]
+            base = res[:, at].astype(F32) if ups == (0,) else merged[:, at]
+            merged[:, at] = base + dot(w, jnp.concatenate(t, axis=0), NN)
             return carry
 
         lax.fori_loop(0, ROWS // GRAD_LANES, step, 0)
 
-    for s in range(2):
-        ring_send(True, 0, s)
-        ring_send(False, 0, s)
-
+    loads[3].wait()
+    own_ex = go(copy(gbuf.at[mp], gbuf.at[mp], esend.at[1], cown, sibling))
+    w_ex = go(copy(wq.at[1 - c], wqin, esend.at[0], erecv.at[0], sibling))
+    w_ex.wait_recv()
+    wqh[...] = wq[c] + wqin[...]
+    for d in FAR_Y:
+        i = other(y, d, NY)
+        go(copy(wqh.at[:, pl.ds(pl.multiple_of(i * PAIR, PAIR), PAIR)], wqr.at[y], wsend.at[d], wrecv.at[y], at_y(i)))
+
+    ring_out(0, 0)
     loads[4].wait()
     rq[...] = sum3(dot(q3, res[...], NN)).reshape(NC, HALF, ROWS)
     r_ex = go(copy(rq.at[1 - c], rqin, esend.at[2], erecv.at[1], sibling))
@@ -218,6 +216,7 @@
     for d in range(1, NY):
         i = other(y, d, NY)
         copy(wqr.at[i], wqr.at[i], wsend.at[d], wrecv.at[i], sibling).wait_recv()
+    ring_out(0, 1)
     w_tok = wqr[0]
     for i in range(1, NY):
         w_tok = w_tok + wqr[i]
@@ -235,8 +234,8 @@
     for n, (dx, dz) in enumerate(FAR_PLANE):
         i = offset(dx, dz)
         go(copy(ps.at[i], pr.at[dp], psend.at[n], precv.at[dp], at_dp(i)))
-    ring_step(1, 0)
-    ring_step(1, 1)
+    grad((0,), ())
+    ring_in(1, 0)
     pr[dp] = ps[dp]
     for dx, dz in FAR_PLANE[::-1]:
         i = offset(dx, dz)
@@ -245,10 +244,9 @@
     for d in FAR_Y:
         i = other(y, d, NY)
         go(copy(yr.at[y], yr.at[y], ysend.at[d], yrecv.at[y], at_y(i)))
-    ring_step(2, 0)
-    ring_step(2, 1)
+    ring_in(1, 1)
     ring_sibling(1)
-    grad(1, 1, first=True)
+    grad((1,), (1,))
     for d in range(1, NY):
         i = other(y, d, NY)
         copy(yr.at[i], yr.at[i], ysend.at[d], yrecv.at[i], sibling).wait_recv()
@@ -256,10 +254,10 @@
     for n, (dx, dz) in enumerate(FAR_PLANE):
         i = offset(dx, dz)
         go(copy(pg.at[dp], pg.at[dp], pgsend.at[n], pgrecv.at[dp], at_dp(i)))
-    ring_step(3, 0)
-    ring_step(3, 1)
-    ring_sibling(2)
-    grad(2, 2)
+    ring_out(1, 0)
+    ring_out(1, 1)
+    ring_in(2, 0)
+    ring_out(2, 0)
     for dx, dz in FAR_PLANE[::-1]:
         i = offset(dx, dz)
         copy(pg.at[i], pg.at[i], pgsend.at[0], pgrecv.at[i], sibling).wait_recv()
@@ -267,28 +265,47 @@
         for k in range(NZ):
             pt[c, ZR * k : ZR * (k + 1), XL * i : XL * (i + 1)] = pg[i * NZ + k]
     go(copy(pt.at[c], pt.at[c], esend.at[3], erecv.at[2], sibling))
-    ring_step(4, 0)
-    ring_step(4, 1)
-    ring_sibling(3)
-    ring_sibling(4)
     copy(pt.at[1 - c], pt.at[1 - c], esend.at[3], erecv.at[2], sibling).wait_recv()
 
     p = pt[...].reshape(RANK, ROWS)
     p3 = split3(p)
-    tokens = gbuf[...].reshape(TOK, ROWS)
-    u3 = split3(sum3(dot(p3, tokens, NT)))
-    q_part = sum3(dot(u3, wbuf[...], NT)) + sum3(dot(p3, res[...], NT))
-    qb[...] = jnp.concatenate([q_part, jnp.zeros((RANK, QL - COLS), F32)], axis=1)
+
+    def chip_lanes(i):
+        return pl.ds(pl.multiple_of(i * PAIR, PAIR), PAIR)
+
+    def tokens_p(i):
+        ubuf[:, chip_lanes(i)] = sum3(dot(p3, gbuf[pl.ds(i * NC, NC)].reshape(PAIR, ROWS), NT))
+
+    tokens_p(y)
+    own_u = ubuf.at[:, chip_lanes(y)]
+    for d in FAR_U:
+        go(copy(own_u, own_u, usend.at[d], urecv.at[d], at_y(other(y, d, NY))))
+    qb[...] = jnp.zeros_like(qb)
+    qb[:, :COLS] = sum3(dot(p3, res[...], NT))
+    tokens_p(other(y, 1, NY))
+    tokens_p(other(y, NY - 1, NY))
+    ring_in(2, 1)
+    ring_out(2, 1)
+    ring_sibling(2)
+    tokens_p(other(y, 2, NY))
+    tokens_p(other(y, NY - 2, NY))
+    for d in FAR_U:
+        theirs = ubuf.at[:, chip_lanes(other(y, NY - d, NY))]
+        copy(theirs, theirs, usend.at[d], urecv.at[d], sibling).wait_recv()
+    qb[:, :COLS] += sum3(dot(split3(ubuf[...]), wbuf[...], NT))
     for d in FAR_X:
         i = other(x, d, NX)
         go(copy(qb.at[pl.ds(pl.multiple_of(i * QR, QR), QR)], qxr.at[x], qxsend.at[d], qxrecv.at[x], at_x(i)))
 
-    grad(3, 3)
-    grad(0, 4)
+    ring_in(3, 0)
+    ring_out(3, 0)
+    inv[...] = inverse_factor(dot_exact(p, p, NT))
     qxr[x] = qb[pl.ds(pl.multiple_of(x * QR, QR), QR), :]
     for d in range(1, NX):
         i = other(x, d, NX)
         copy(qxr.at[i], qxr.at[i], qxsend.at[d], qxrecv.at[i], sibling).wait_recv()
+    ring_in(3, 1)
+    ring_out(3, 1)
     total = qxr[0]
     for i in range(1, NX):
         total = total + qxr[i]
@@ -296,7 +313,9 @@
     for d in FAR_Z:
         i = other(z, d, NZ)
         go(copy(qzr.at[z], qzr.at[z], qzsend.at[d], qzrecv.at[z], at_z(i)))
-    inv = inverse_factor(dot_exact(p, p, NT))
+    grad((2,), (2,))
+    ring_sibling(3)
+    grad((3,), (3,))
     for d in range(1, NZ):
         i = other(z, d, NZ)
         copy(qzr.at[i], qzr.at[i], qzsend.at[d], qzrecv.at[i], sibling).wait_recv()
@@ -307,11 +326,15 @@
     for d in FAR_X:
         i = other(x, d, NX)
         go(copy(qt.at[x], qt.at[x], qgsend.at[d], qgrecv.at[x], at_x(i)))
-    phat_ref[...] = dot_exact(inv, p, NN)
+    phat_ref[...] = dot_exact(inv[...], p, NN)
+    ring_in(4, 0)
+    ring_in(4, 1)
+    ring_sibling(4)
+    grad((), (4,))
     for d in range(1, NX):
         i = other(x, d, NX)
         copy(qt.at[i], qt.at[i], qgsend.at[d], qgrecv.at[i], sibling).wait_recv()
-    qnext_ref[...] = dot_exact(inv, qt[...].reshape(RANK, QL), NN)
+    qnext_ref[...] = dot_exact(inv[...], qt[...].reshape(RANK, QL), NN)
     for cp in pending:
         cp.wait_send()
 
@@ -355,6 +378,8 @@
             vmem((NX, QR, QL), F32),
             vmem((NZ, QR, QL), F32),
             vmem((NX, QR, QL), F32),
+            vmem((RANK, RANK), F32),
+            vmem((RANK, TOK), F32),
             dma((5,)),
             dma((2, 4, 2)), dma((2, 4, 2)),
             dma((2, 4, 2)), dma((2, 4, 2)),
@@ -368,6 +393,7 @@
             dma((NX,)), dma((NX,)),
             dma((NZ,)), dma((NZ,)),
             dma((NX,)), dma((NX,)),
+            dma((NY,)), dma((NY,)),
         ],
         compiler_params=pltpu.CompilerParams(
             collective_id=0, has_side_effects=True, vmem_limit_bytes=40 << 20

time: 70.7 us -> 67.5 us (0.955)
  Pallas kernels: 69.9 us -> 66.7 us
    pallas_call x1, Pallas kernels: 68.2 us -> 64.9 us  [chain(): pl.pallas_call(chain_kernel, out_shape=(vmem((COLS, ROWS), F32), vmem((RA...]
where the time goes in v3:
time: 67.5 us; the launch traced here: 67.4 us
  Pallas kernels  66.7 us (99%)
    pallas_call x1, Pallas kernels, chain(): pl.pallas_call(chain_kernel, out_shape=(vmem((COLS, ROWS), F32), vmem((RA...  64.9 us
    pallas_call x1, Pallas kernels, final(): pl.pallas_call(final_kernel, out_shape=tuple((jax.ShapeDtypeStruct(*s) fo...  1.79 us

profile of v3, /device:TPU:1, one launch (start us, length us, event | category | flops | bytes accessed | tf_op | source)
XLA Modules:
  0.0 67.4 jit_solution(8096899592531485684)
XLA Ops:
  0.6 64.9 %chain.1 = (f32[320,2560]{1,0:T(8,128)S(1)}, f32[32,2560]{1,0:T(8,128)S(1)}, f32[32,384]{1,0:T(8,128)S(1)}) custom-call(bf16[64,2560]{1,0:T(8,128)(2,1)} %bitcast.14, bf16[320,1024]{1,0:T(8,128)(2,1)} %bitcast.13, s32[1,1024]{1,0:T(1,128)} %cnt_hbm.1, bf16[320,2560]{1,0:T(8,128)(2,1)} %bitcast.12, f32[32,320]{1,0:T(8,128)} %bitcast.15), custom_call_target="tpu_custom_call" | custom-call | tf_op jit(solution)/shard_map/chain/pallas_call | solution.py:345
  65.6 1.8 %final.1 = (bf16[80,320]{1,0:T(8,128)(2,1)}, bf16[320,2560]{1,0:T(8,128)(2,1)}, f32[32,320]{1,0:T(8,128)}) custom-call(f32[320,2560]{1,0:T(8,128)S(1)} %get-tuple-element.9.merged_ref, f32[32,2560]{1,0:T(8,128)S(1)} %get-tuple-element.10.phat_ref, f32[32,384]{1,0:T(8,128)S(1)} %get-tuple-element.11.qnext_ref), custom_call_target="tpu_custom_call" | custom-call | tf_op jit(solution)/shard_map/final/pallas_call | solution.py:445

commit v4 on v3

--- a/solution.py
+++ b/solution.py
@@ -19,7 +19,8 @@
 QR = RANK // NX
 QL = 384
 SUB = BLOCK // 2
-GRAD_LANES = 640
+PANEL = 4
+GRAD_LANES = 1280
 
 
 def far_first(*sizes):
@@ -67,11 +68,15 @@
     work = jnp.concatenate([gram, jnp.zeros((RANK, 128 - RANK), F32)], axis=1) + eye
 
     pivots = jnp.ones((RANK, 128), F32)
-    for j in range(RANK):
-        col = jnp.broadcast_to(work[:, j : j + 1], (RANK, 128))
-        pivot = col[j : j + 1]
-        pivots = jnp.where(rows == j, pivot, pivots)
-        work = jnp.where(rows > j, work - col * (work[j : j + 1] / pivot), work)
+    for first in range(0, RANK, PANEL):
+        cols = [jnp.broadcast_to(work[:, j : j + 1], (RANK, 128)) for j in range(first, first + PANEL)]
+        for k in range(PANEL):
+            j = first + k
+            pivot = cols[k][j : j + 1]
+            pivots = jnp.where(rows == j, pivot, pivots)
+            below = jnp.where(rows > j, cols[k], 0.0) * (1.0 / pivot)
+            work = work - below * work[j : j + 1]
+            cols = [cols[m] - below * cols[m][j : j + 1] if m > k else cols[m] for m in range(PANEL)]
     return (work / jnp.sqrt(pivots))[:, RANK : 2 * RANK]
 
 
@@ -234,8 +239,9 @@
     for n, (dx, dz) in enumerate(FAR_PLANE):
         i = offset(dx, dz)
         go(copy(ps.at[i], pr.at[dp], psend.at[n], precv.at[dp], at_dp(i)))
+    ring_in(1, 0)
+    ring_out(1, 0)
     grad((0,), ())
-    ring_in(1, 0)
     pr[dp] = ps[dp]
     for dx, dz in FAR_PLANE[::-1]:
         i = offset(dx, dz)
@@ -254,7 +260,6 @@
     for n, (dx, dz) in enumerate(FAR_PLANE):
         i = offset(dx, dz)
         go(copy(pg.at[dp], pg.at[dp], pgsend.at[n], pgrecv.at[dp], at_dp(i)))
-    ring_out(1, 0)
     ring_out(1, 1)
     ring_in(2, 0)
     ring_out(2, 0)

time: 67.5 us -> 63.3 us (0.938)
  Pallas kernels: 66.7 us -> 62.5 us
    pallas_call x1, Pallas kernels: 64.9 us -> 60.7 us  [chain(): pl.pallas_call(chain_kernel, out_shape=(vmem((COLS, ROWS), F32), vmem((RA...]
where the time goes in v4:
time: 63.3 us; the launch traced here: 63.1 us
  Pallas kernels  62.5 us (99%)
  between operations  0.64 us (1%)
    pallas_call x1, Pallas kernels, chain(): pl.pallas_call(chain_kernel, out_shape=(vmem((COLS, ROWS), F32), vmem((RA...  60.7 us
    pallas_call x1, Pallas kernels, final(): pl.pallas_call(final_kernel, out_shape=tuple((jax.ShapeDtypeStruct(*s) fo...  1.79 us

profile of v4, /device:TPU:1, one launch (start us, length us, event | category | flops | bytes accessed | tf_op | source)
XLA Modules:
  0.0 63.1 jit_solution(6588986088435559419)
XLA Ops:
  0.6 60.7 %chain.1 = (f32[320,2560]{1,0:T(8,128)S(1)}, f32[32,2560]{1,0:T(8,128)S(1)}, f32[32,384]{1,0:T(8,128)S(1)}) custom-call(bf16[64,2560]{1,0:T(8,128)(2,1)} %bitcast.14, bf16[320,1024]{1,0:T(8,128)(2,1)} %bitcast.13, s32[1,1024]{1,0:T(1,128)} %cnt_hbm.1, bf16[320,2560]{1,0:T(8,128)(2,1)} %bitcast.12, f32[32,320]{1,0:T(8,128)} %bitcast.15), custom_call_target="tpu_custom_call" | custom-call | tf_op jit(solution)/shard_map/chain/pallas_call | solution.py:350
  61.4 1.8 %final.1 = (bf16[80,320]{1,0:T(8,128)(2,1)}, bf16[320,2560]{1,0:T(8,128)(2,1)}, f32[32,320]{1,0:T(8,128)}) custom-call(f32[320,2560]{1,0:T(8,128)S(1)} %get-tuple-element.9.merged_ref, f32[32,2560]{1,0:T(8,128)S(1)} %get-tuple-element.10.phat_ref, f32[32,384]{1,0:T(8,128)S(1)} %get-tuple-element.11.qnext_ref), custom_call_target="tpu_custom_call" | custom-call | tf_op jit(solution)/shard_map/final/pallas_call | solution.py:450

commit v5 on v4

--- a/solution.py
+++ b/solution.py
@@ -123,16 +123,17 @@
         pltpu.make_async_copy(inp_hbm, gbuf.at[mp], lsem.at[3]),
         pltpu.make_async_copy(res_hbm, res, lsem.at[4]),
     ]
-    for load in loads:
+    for load in loads[:3]:
         load.start()
 
     barrier = pltpu.get_barrier_semaphore()
-    peers = [sibling]
+    peers = [at_y(other(y, d, NY)) for d in FAR_Y] + [sibling]
     peers += [at_x(other(x, d, NX)) for d in range(1, NX)]
     peers += [at_z(other(z, d, NZ)) for d in range(1, NZ)]
-    peers += [at_y(other(y, d, NY)) for d in range(1, NY)]
     for peer in peers:
         pl.semaphore_signal(barrier, inc=1, device_id=peer, device_id_type=MESH)
+    for load in loads[3:]:
+        load.start()
 
     loads[0].wait()
     loads[1].wait()

time: 63.3 us -> 63.4 us (level)
  no operation moved by 1% of the time
where the time goes in v5:
time: 63.4 us; the launch traced here: 63.2 us
  Pallas kernels  62.6 us (99%)
  between operations  0.64 us (1%)
    pallas_call x1, Pallas kernels, chain(): pl.pallas_call(chain_kernel, out_shape=(vmem((COLS, ROWS), F32), vmem((RA...  60.8 us
    pallas_call x1, Pallas kernels, final(): pl.pallas_call(final_kernel, out_shape=tuple((jax.ShapeDtypeStruct(*s) fo...  1.79 us

profile of v5, /device:TPU:1, one launch (start us, length us, event | category | flops | bytes accessed | tf_op | source)
XLA Modules:
  0.0 63.2 jit_solution(6072596252278129992)
XLA Ops:
  0.6 60.8 %chain.1 = (f32[320,2560]{1,0:T(8,128)S(1)}, f32[32,2560]{1,0:T(8,128)S(1)}, f32[32,384]{1,0:T(8,128)S(1)}) custom-call(bf16[64,2560]{1,0:T(8,128)(2,1)} %bitcast.14, bf16[320,1024]{1,0:T(8,128)(2,1)} %bitcast.13, s32[1,1024]{1,0:T(1,128)} %cnt_hbm.1, bf16[320,2560]{1,0:T(8,128)(2,1)} %bitcast.12, f32[32,320]{1,0:T(8,128)} %bitcast.15), custom_call_target="tpu_custom_call" | custom-call | tf_op jit(solution)/shard_map/chain/pallas_call | solution.py:351
  61.4 1.8 %final.1 = (bf16[80,320]{1,0:T(8,128)(2,1)}, bf16[320,2560]{1,0:T(8,128)(2,1)}, f32[32,320]{1,0:T(8,128)}) custom-call(f32[320,2560]{1,0:T(8,128)S(1)} %get-tuple-element.9.merged_ref, f32[32,2560]{1,0:T(8,128)S(1)} %get-tuple-element.10.phat_ref, f32[32,384]{1,0:T(8,128)S(1)} %get-tuple-element.11.qnext_ref), custom_call_target="tpu_custom_call" | custom-call | tf_op jit(solution)/shard_map/final/pallas_call | solution.py:451
